TPU v7x, 32 devices: a whole 2x2x4 slice. The times are simulated.
32 devices in a mesh: grp: 8 (over z, y), blk: 4 (over x, core).
Axes of the slice: x: 2, y: 2, z: 4, core: 2. Of those that a mesh axis runs over, the one named last changes fastest.
Arguments:
- states: bfloat16 [65536, 768], P(('grp', 'blk')), may hold values from -6 to 6
- query_weight: bfloat16 [768, 768], replicated, may hold values from -0.21875 to 0.21875
- attempts: bfloat16 [2048, 768], P(('grp', 'blk')), may hold values from -6 to 6
- attempt_theorem: int32 [2048], P('grp'), may hold values from 0 to 15
- positive: int32 [65536], P(('grp', 'blk')), may hold values from 0 to 255
Outputs:
- loss: float32 [65536], P(('grp', 'blk'))
- grad_attempts: float32 [2048, 768], P(('grp', 'blk'))
- grad_weight: float32 [768, 768], replicated
All inputs are finite; a program needn't handle non-finite values.
Results may differ from a plain program's by a relative error of at most 0.012.
Values may be sent and summed in bfloat16 or wider, within the bound.
A program may use at most 64 MiB of HBM per device.

v0:
```python
import jax
import jax.numpy as jnp
from jax import lax
from jax.sharding import PartitionSpec as P

logit_sharpness = 0.07
epsilon = 1e-06


def normalized_rows(values):
    return values * lax.rsqrt(jnp.mean(values * values, axis=-1, keepdims=True) + epsilon)


def on_device(states, query_weight, attempts, attempt_theorem, positive):
    vector_dimension = states.shape[1]
    logit_multiplier = 1.0 / (logit_sharpness * vector_dimension)
    attempt_rows_float, attempt_back = jax.vjp(normalized_rows, attempts.astype(jnp.float32))
    candidate_direction = attempt_rows_float.astype(jnp.bfloat16)
    proj = jnp.dot(states, query_weight, preferred_element_type=jnp.float32)
    query_float, query_back = jax.vjp(normalized_rows, proj)
    query_unit = query_float.astype(jnp.bfloat16)
    anchor_lemma_label = jnp.take(attempt_theorem, positive)
    panel = lax.all_gather(candidate_direction, "blk", axis=0, tiled=True)
    scores = (
        lax.dot_general(
            query_unit, panel, (((1,), (1,)), ((), ())), preferred_element_type=jnp.float32
        )
        * logit_multiplier
    )
    mask = anchor_lemma_label[:, None] == attempt_theorem[None, :]
    expo = jnp.where(mask, jnp.exp(scores), 0.0)
    total = jnp.sum(expo, axis=1)
    columns = lax.broadcasted_iota(jnp.int32, scores.shape, 1)
    chosen = columns == positive[:, None]
    pos_score = jnp.sum(jnp.where(chosen, scores, 0.0), axis=1)
    losses = jnp.log(total) - pos_score
    weights = (expo / total[:, None] - chosen.astype(jnp.float32)).astype(jnp.bfloat16)
    grad_qunit = jnp.dot(weights, panel, preferred_element_type=jnp.float32) * logit_multiplier
    grad_aunit = lax.psum_scatter(
        (
            lax.dot_general(
                weights, query_unit, (((0,), (0,)), ((), ())), preferred_element_type=jnp.float32
            )
            * logit_multiplier
        ).astype(jnp.bfloat16),
        "blk",
        scatter_dimension=0,
        tiled=True,
    ).astype(jnp.float32)
    grad_attempts = attempt_back(grad_aunit)[0]
    grad_proj = query_back(grad_qunit)[0].astype(jnp.bfloat16)
    weight_term = lax.dot_general(
        states, grad_proj, (((0,), (0,)), ((), ())), preferred_element_type=jnp.float32
    )
    grad_weight = lax.psum(weight_term, ("grp", "blk"))
    return (losses, grad_attempts, grad_weight)


def solution(mesh):
    in_specs = (P(("grp", "blk"), None), P(), P(("grp", "blk"), None), P("grp"), P(("grp", "blk")))
    out_specs = (P(("grp", "blk")), P(("grp", "blk"), None), P())
    return jax.shard_map(
        on_device, mesh=mesh, in_specs=in_specs, out_specs=out_specs, check_vma=False
    )
```

profile of v0, /device:TPU:1, one launch (start us, length us, event | category | flops | bytes accessed | tf_op | source)
XLA Modules:
  0.0 195.8 jit_solution(55276423248281277)
XLA Ops:
  8.0 0.0 copy-start
  8.0 0.0 copy-start.1
  8.0 0.0 reduce-scatter.2.cloned.1.call-start
  8.1 1.2 fusion.10
  9.2 0.7 fusion.14
  10.0 0.0 copy-done.1
  10.0 0.0 copy-start.4
  10.0 0.0 copy-start.2
  10.0 13.2 %gather_fusion = s32[2048]{0:T(1024)S(1)} fusion(s32[256]{0:T(256)S(1)} %copy-done.1, s32[2048]{0:T(1024)S(1)} %fusion.14), kind=kCustom, calls=%fused_computation | custom fusion | bytes 24576 | tf_op jit(solution)/shard_map/jit(_take)/gather | solution.py:22
  23.2 0.0 copy-done.4
  23.2 0.0 copy-done.2
  23.2 0.1 fusion.11
  23.3 7.8 %all_gather.3 = bf16[256,768]{1,0:T(8,128)(2,1)S(1)} all-gather(bf16[64,768]{1,0:T(8,128)(2,1)S(1)} %fusion.11), channel_id=1, replica_groups=mesh['grp'=8,'blk'=4] {'blk'}, dimensions={0}, use_global_device_ids=true | all-gather | bytes 491520 | tf_op jit(solution)/shard_map/all_gather | solution.py:23
  31.1 0.0 copy-done
  31.1 0.0 copy-start.3
  31.1 4.2 %multiply_reduce_fusion.1 = (f32[2048]{0:T(1024)S(1)}, f32[2048,768]{0,1:T(8,128)S(1)}) fusion(bf16[2048,768]{1,0:T(8,128)(2,1)S(1)} %copy-done, bf16[768,768]{1,0:T(8,128)(2,1)} %param.6), kind=kOutput, calls=%fused_computation.5 | convolution fusion | flops 2419062784 | bytes 10625024 | tf_op jit(solution)/shard_map/dot_general | solution.py:19
  35.3 0.0 copy-start.5
  35.4 0.0 copy-done.3
  35.4 1.5 fusion.5
  36.9 0.0 copy-start.7
  36.9 1.1 copy-done.5
  38.0 0.7 copy-done.7
  38.7 2.3 %fusion.9 = bf16[256,768]{1,0:T(8,128)(2,1)} fusion(f32[2048,768]{0,1:T(8,128)S(1)} %get-tuple-element.14, f32[2048]{0:T(1024)S(1)} %fusion.13, f32[2048,256]{0,1:T(8,128)S(1)} %get-tuple-element.15, f32[2048]{0:T(1024)S(1)} %get-tuple-element.9, s32[2048]{0:T(1024)S(1)} %copy-done.4, s32[2048]{0:T(1024)S(1)} %and_select_fusion, s32[256]{0:T(256)S(1)} %copy-done.1), kind=kOutput, calls=%fused_computation.17 | convolution fusion | flops 812515328 | bytes 8815616 | tf_op jit(solution)/shard_map/dot_general | solution.py:41
  41.0 0.0 reduce-scatter.2.cloned.1.call-update
  41.1 0.0 all-reduce.2.cloned.1.call-start
  41.1 0.0 copy-start.6
  41.1 5.4 %multiply_reduce_fusion = (f32[2048]{0:T(1024)S(1)}, f32[2048,768]{0,1:T(8,128)S(1)}) fusion(f32[2048,768]{0,1:T(8,128)} %copy-done.5, bf16[256,768]{1,0:T(8,128)(2,1)} %copy-done.3, f32[2048,256]{0,1:T(8,128)} %copy-done.7, f32[2048]{0:T(1024)S(1)} %get-tuple-element.9, s32[2048]{0:T(1024)S(1)} %copy-done.4, s32[2048]{0:T(1024)S(1)} %and_select_fusion, ...), kind=kOutput, calls=%fused_computation.3 | convolution fusion | flops 813692928 | bytes 15107072 | tf_op jit(solution)/shard_map/dot_general | solution.py:38
  46.5 0.0 copy-done.6
  46.5 4.3 %fusion.6 = f32[768,768]{0,1:T(8,128)} fusion(bf16[2048,768]{1,0:T(8,128)(2,1)S(1)} %copy-done, f32[2048,768]{0,1:T(8,128)S(1)} %copy-done.6, f32[2048,768]{0,1:T(8,128)S(1)} %get-tuple-element.17, f32[2048]{0:T(1024)S(1)} %get-tuple-element.12, f32[2048]{0:T(1024)S(1)} %get-tuple-element.11), kind=kOutput, calls=%fused_computation.15 | convolution fusion | flops 2423783424 | bytes 18104320 | tf_op jit(solution)/shard_map/dot_general | solution.py:52
  50.9 0.0 all-reduce.2.cloned.1.call-update
  50.9 0.6 log_subtract_fusion
  51.5 11.9 %reduce-scatter.2.cloned.1.call-done = bf16[64,768]{1,0:T(8,128)(2,1)} async-done(((bf16[256,768]{1,0:T(8,128)(2,1)}), bf16[64,768]{1,0:T(8,128)(2,1)}) %reduce-scatter.2.cloned.1.call-update) | async-done | bytes 98320 | tf_op jit(solution)/shard_map/reduce_scatter | solution.py:39
  63.4 1.0 fusion.12
  64.4 1.7 add_add_fusion.1
  66.1 119.2 %all-reduce.2.cloned.1.call-done = f32[768,768]{0,1:T(8,128)} async-done(((f32[768,768]{0,1:T(8,128)}), f32[768,768]{0,1:T(8,128)}) %all-reduce.2.cloned.1.call-update) | async-done | bytes 2359312 | tf_op jit(solution)/shard_map/psum | solution.py:55
  185.3 3.0 %copy.9 = f32[768,768]{1,0:T(8,128)} copy(f32[768,768]{0,1:T(8,128)} %all-reduce.2.cloned.1.call-done) | data formatting | bytes 4718592
  (5 shorter events, 0.0 us)
Async XLA Ops:
  8.0 23.1 %copy-start = (bf16[2048,768]{1,0:T(8,128)(2,1)S(1)}, bf16[2048,768]{1,0:T(8,128)(2,1)}, u32[]{:S(2)}) copy-start(bf16[2048,768]{1,0:T(8,128)(2,1)} %param.5) | copy-start | bytes 9437188
  8.0 1.9 copy-start.1
  8.0 55.4 %reduce-scatter.2.cloned.1.call-start = ((), (), s32[]{:S(2)}) async-start(), calls=%async_computation.1 | async-start | bytes 491520 | tf_op jit(solution)/shard_map/reduce_scatter | solution.py:39
  10.0 13.2 %copy-start.4 = (s32[2048]{0:T(1024)S(1)}, s32[2048]{0:T(1024)}, u32[]{:S(2)}) copy-start(s32[2048]{0:T(1024)} %param.9) | copy-start | bytes 24580
  10.0 13.2 %copy-start.2 = (bf16[64,768]{1,0:T(8,128)(2,1)S(1)}, bf16[64,768]{1,0:T(8,128)(2,1)}, u32[]{:S(2)}) copy-start(bf16[64,768]{1,0:T(8,128)(2,1)} %param.7) | copy-start | bytes 294916
  31.1 4.2 %copy-start.3 = (bf16[256,768]{1,0:T(8,128)(2,1)}, bf16[256,768]{1,0:T(8,128)(2,1)S(1)}, u32[]{:S(2)}) copy-start(bf16[256,768]{1,0:T(8,128)(2,1)S(1)} %all_gather.3) | copy-start | bytes 1179652
  35.3 2.7 %copy-start.5 = (f32[2048,768]{0,1:T(8,128)}, f32[2048,768]{0,1:T(8,128)S(1)}, u32[]{:S(2)}) copy-start(f32[2048,768]{0,1:T(8,128)S(1)} %get-tuple-element.14) | copy-start | bytes 18874372
  36.9 1.8 copy-start.7
  41.1 144.3 %all-reduce.2.cloned.1.call-start = ((), (), s32[]{:S(2)}) async-start(), calls=%async_computation.2 | async-start | bytes 4718592 | tf_op jit(solution)/shard_map/psum | solution.py:55
  41.1 5.4 %copy-start.6 = (f32[2048,768]{0,1:T(8,128)S(1)}, f32[2048,768]{0,1:T(8,128)}, u32[]{:S(2)}) copy-start(f32[2048,768]{0,1:T(8,128)} %copy-done.5) | copy-start | bytes 18874372
Sparse Core Ops, SparseCore 0:
  41.2 22.1 reduce-scatter.1
Sparse Core Ops, SparseCore 1:
  51.0 134.3 all-reduce.1
where the time goes:
time: 198 us; the launch traced here: 196 us
  waiting for transfers between devices  131 us (66%)
  local copies, waits for them, and re-layouts  18.1 us (9%)
  matrix products  17.8 us (9%)
  between operations  15.6 us (8%)
  blocking collectives  7.8 us (4%)
  other arithmetic  5.33 us (3%)
    psum x1, waiting for transfers between devices, on_device(): grad_weight = lax.psum(weight_term, ('grp', 'blk'))  119 us
    gather x1, local copies, waits for them, and re-layouts, on_device(): anchor_lemma_label = jnp.take(attempt_theorem, positive)  13.2 us
    reduce_scatter x1, waiting for transfers between devices, on_device(): lax.psum_scatter((lax.dot_general(weights, query_unit, (((0,), (0,)), (()...  11.9 us
    all_gather x1, blocking collectives, on_device(): panel = lax.all_gather(candidate_direction, 'blk', axis=0, tiled=True)  7.8 us
    dot_general x1, matrix products, on_device(): jnp.dot(weights, panel, preferred_element_type=jnp.float32)  5.38 us
    unnamed x17, local copies, waits for them, and re-layouts  4.92 us
    dot_general x1, matrix products, on_device(): lax.dot_general(states, grad_proj, (((0,), (0,)), ((), ())), preferred_el...  4.34 us
    dot_general x1, matrix products, on_device(): proj = jnp.dot(states, query_weight, preferred_element_type=jnp.float32)  4.21 us
  transfers between devices with their start and end apart: 2, of which 2 were waited for; matrix products, arithmetic and copies ran while one was open for 7% of the time, Pallas kernels for 0%

commit v1 on v0

v1 whole, which is shorter than its diff:
```python
import functools

import jax
import jax.numpy as jnp
from jax import lax
from jax.experimental import pallas as pl
from jax.experimental.pallas import tpu as pltpu
from jax.sharding import PartitionSpec as P

logit_sharpness = 0.07
epsilon = 1e-06
MESH = pl.DeviceIdType.MESH
PARTS = 3
LANES = 128
TILE = 16
NT = (((1,), (1,)), ((), ()))


def stage_plan(n_grp, n_blk, rows):
    along_x = ("blk", 2, n_blk // 2)
    along_y = ("grp", 1, 2)
    along_z = ("grp", 2, n_grp // 2)
    orders = (
        (along_x, along_y, along_z),
        (along_y, along_z, along_x),
        (along_z, along_x, along_y),
    )
    plan = []
    for order in orders:
        length, stages = rows, []
        for axis, stride, size in order:
            if size == 1:
                continue
            scatter = length % (size * TILE) == 0
            stages.append((axis, stride, size, length, scatter))
            if scatter:
                length //= size
        plan.append(stages)
    return plan


def kernel(
    n_grp, n_blk, plan, chunk,
    states, weight, attempts, theorem, positive,
    loss, grad_att, grad_w,
    weight_t, unit_t, gproj_t, w_all, inv_rms, panel, panel_t,
    ga_stage, ga_recv, acc, core_send, core_recv, res, send_sems, recv_sems, *stage_bufs,
):
    queries, dim = states.shape
    own_att = attempts.shape[0]
    n_att = own_att * n_blk
    half = dim // 2
    width = dim // PARTS
    multiplier = 1.0 / (logit_sharpness * dim)
    grp = lax.axis_index("grp")
    blk = lax.axis_index("blk")
    core = lax.rem(blk, 2)
    sibling = blk + 1 - 2 * core
    used = [0]
    started = []

    def member(axis, stride, size):
        index = grp if axis == "grp" else blk
        return lax.rem(index // stride, size)

    def partner(axis, stride, size, k):
        index = grp if axis == "grp" else blk
        here = lax.rem(index // stride, size)
        there = lax.rem(here + k, size)
        return {axis: index + (there - here) * stride}, there

    def send(src, dst, device):
        n = used[0]
        used[0] += 1
        copy = pltpu.make_async_remote_copy(
            src_ref=src, dst_ref=dst, send_sem=send_sems.at[n], recv_sem=recv_sems.at[n],
            device_id=device, device_id_type=MESH,
        )
        copy.start()
        started.append(copy)
        return copy

    greeted = [("blk", 1, n_blk), ("grp", 1, 2), ("grp", 2, n_grp // 2)]
    barrier = pltpu.get_barrier_semaphore()
    count = 0
    for axis, stride, size in greeted:
        for k in range(1, size):
            pl.semaphore_signal(
                barrier, inc=1, device_id=partner(axis, stride, size, k)[0], device_id_type=MESH
            )
            count += 1

    att = attempts[...].astype(jnp.float32)
    att_r = lax.rsqrt(jnp.mean(att * att, axis=1, keepdims=True) + epsilon)
    att_unit = att * att_r
    own_rows = pl.ds(pl.multiple_of(blk * own_att, own_att), own_att)
    panel[own_rows, :] = att_unit.astype(jnp.bfloat16)
    pl.semaphore_wait(barrier, count)
    gathers = [
        send(panel.at[own_rows], panel.at[own_rows], partner("blk", 1, n_blk, k)[0])
        for k in range(1, n_blk)
    ]

    weight_t[...] = weight[...].T

    def project(step, carry):
        cols = pl.ds(pl.multiple_of(step * chunk, chunk), chunk)
        proj = lax.dot_general(
            weight_t[...], states[cols, :], NT, preferred_element_type=jnp.float32
        )
        r = lax.rsqrt(jnp.sum(proj * proj, axis=0, keepdims=True) * (1.0 / dim) + epsilon)
        inv_rms[:, cols] = r
        unit_t[:, cols] = (proj * r).astype(jnp.bfloat16)
        return carry

    lax.fori_loop(0, queries // chunk, project, 0)

    for copy in gathers:
        copy.wait_recv()
    panel_t[...] = panel[...].T
    theorem_col = jnp.broadcast_to(theorem[...].astype(jnp.float32), (8, n_att)).T[:, 0:1]

    def contrast(step, carry):
        cols = pl.ds(pl.multiple_of(step * chunk, chunk), chunk)
        unit = unit_t[:, cols]
        scores = jnp.dot(panel[...], unit, preferred_element_type=jnp.float32) * multiplier
        chosen = lax.broadcasted_iota(jnp.int32, scores.shape, 0) == positive[:, cols]
        label = jnp.sum(jnp.where(chosen, theorem_col, 0.0), axis=0, keepdims=True)
        expo = jnp.where(theorem_col == label, jnp.exp(scores), 0.0)
        total = jnp.sum(expo, axis=0, keepdims=True)
        pos_score = jnp.sum(jnp.where(chosen, scores, 0.0), axis=0, keepdims=True)
        loss[:, cols] = jnp.log(total) - pos_score
        w = (expo * (1.0 / total) - jnp.where(chosen, 1.0, 0.0)).astype(jnp.bfloat16)
        w_all[:, cols] = w
        along = jnp.sum(w.astype(jnp.float32) * scores, axis=0, keepdims=True) * (1.0 / dim)
        r = inv_rms[:, cols]
        g = jnp.dot(panel_t[...], w, preferred_element_type=jnp.float32)
        gproj_t[:, cols] = (
            g * (r * multiplier) - unit.astype(jnp.float32) * (r * along)
        ).astype(jnp.bfloat16)
        return carry

    lax.fori_loop(0, queries // chunk, contrast, 0)

    ga_t = lax.dot_general(unit_t[...], w_all[...], NT, preferred_element_type=jnp.float32)
    ga_stage[...] = (ga_t * multiplier).T.astype(jnp.bfloat16)
    ga_copies = []
    for k in range(1, n_blk):
        device, owner = partner("blk", 1, n_blk, k)
        rows = pl.ds(pl.multiple_of(owner * own_att, own_att), own_att)
        ga_copies.append(send(ga_stage.at[rows], ga_recv.at[k - 1], device))

    def weight_tile(which, part):
        rows = pl.ds(pl.multiple_of(which * half, half), half)
        tile = jnp.dot(
            gproj_t[rows, :], states[:, part * width:(part + 1) * width],
            preferred_element_type=jnp.float32,
        )
        return tile.T

    blocks = half // LANES
    bufs = [[None] * len(stages) for stages in plan]
    n = 0
    for part, stages in enumerate(plan):
        for j in range(len(stages)):
            bufs[part][j] = (stage_bufs[n], stage_bufs[n + 1])
            n += 2
    begin = [0] * PARTS
    pending = {}

    def start_stage(part, j):
        axis, stride, size, length, scatter = plan[part][j]
        stage, recv = bufs[part][j]
        here = member(axis, stride, size)
        now = begin[part]
        rows = pl.ds(pl.multiple_of(now, TILE), length)
        stage[...] = acc[part, rows, :].astype(jnp.bfloat16)
        copies = []
        for k in range(1, size):
            device, there = partner(axis, stride, size, k)
            if scatter:
                piece = length // size
                src = stage.at[pl.ds(pl.multiple_of(there * piece, TILE), piece)]
                copies.append(send(src, recv.at[k - 1], device))
            else:
                copies.append(send(stage, recv.at[here], device))
        pending[part, j] = copies

    def finish_stage(part, j):
        axis, stride, size, length, scatter = plan[part][j]
        stage, recv = bufs[part][j]
        here = member(axis, stride, size)
        for copy in pending[part, j]:
            copy.wait_recv()
        if scatter:
            piece = length // size
            begin[part] = begin[part] + here * piece
            rows = pl.ds(pl.multiple_of(begin[part], TILE), piece)
            total = acc[part, rows, :]
            for k in range(size - 1):
                total = total + recv[k].astype(jnp.float32)
        else:
            rows = pl.ds(pl.multiple_of(begin[part], TILE), length)
            recv[here] = stage[...]
            total = recv[0].astype(jnp.float32)
            for k in range(1, size):
                total = total + recv[k].astype(jnp.float32)
        acc[part, rows, :] = total

    sequence = (2, 0, 1)
    core_copies = {}
    for part in sequence:
        tile = weight_tile(1 - core, part)
        for e in range(blocks):
            core_send[part, e * width:(e + 1) * width, :] = (
                tile[:, e * LANES:(e + 1) * LANES].astype(jnp.bfloat16)
            )
        core_copies[part] = send(core_send.at[part], core_recv.at[part], {"blk": sibling})
    for part in sequence:
        tile = weight_tile(core, part)
        core_copies[part].wait_recv()
        for e in range(blocks):
            span = slice(e * width, (e + 1) * width)
            acc[part, span, :] = (
                tile[:, e * LANES:(e + 1) * LANES] + core_recv[part, span, :].astype(jnp.float32)
            )
        start_stage(part, 0)

    for copy in ga_copies:
        copy.wait_recv()
    ga = ga_stage[own_rows, :].astype(jnp.float32)
    for k in range(n_blk - 1):
        ga = ga + ga_recv[k].astype(jnp.float32)
    att = attempts[...].astype(jnp.float32)
    att_r = lax.rsqrt(jnp.mean(att * att, axis=1, keepdims=True) + epsilon)
    att_unit = att * att_r
    grad_att[...] = att_r * (ga - att_unit * jnp.mean(ga * att_unit, axis=1, keepdims=True))

    depth = len(plan[0])
    for j in range(depth):
        for part in sequence:
            finish_stage(part, j)
            if j + 1 < depth:
                start_stage(part, j + 1)

    where = {}
    for part in sequence:
        length = plan[part][0][3]
        for axis, stride, size, rows_in, scatter in plan[part]:
            length = rows_in // size if scatter else rows_in
        rows = pl.ds(pl.multiple_of(begin[part], TILE), length)
        res[core, part, rows, :] = acc[part, rows, :].astype(jnp.bfloat16)
        where[part] = begin[part]
    for j in reversed(range(depth)):
        for part in sequence:
            axis, stride, size, length, scatter = plan[part][j]
            if not scatter:
                continue
            piece = length // size
            rows = pl.ds(pl.multiple_of(where[part], TILE), piece)
            for later in range(j + 1, depth):
                for copy in pending.pop(("back", part, later), []):
                    copy.wait_recv()
            spot = res.at[core, part, rows]
            pending["back", part, j] = [
                send(spot, spot, partner(axis, stride, size, k)[0]) for k in range(1, size)
            ]
            where[part] = where[part] - member(axis, stride, size) * piece
    last = {}
    for part in sequence:
        for key in [key for key in pending if key[0] == "back" and key[1] == part]:
            for copy in pending.pop(key):
                copy.wait_recv()
        spot = res.at[core, part]
        last[part] = send(spot, spot, {"blk": sibling})

    def place(which, part):
        for e in range(blocks):
            cols = pl.ds(pl.multiple_of(which * half + e * LANES, LANES), LANES)
            grad_w[part * width:(part + 1) * width, cols] = (
                res[which, part, e * width:(e + 1) * width, :]
            )

    for part in sequence:
        place(core, part)
    for part in sequence:
        last[part].wait_recv()
        place(1 - core, part)
    for copy in started:
        copy.wait_send()


def on_device(n_grp, n_blk, states, query_weight, attempts, attempt_theorem, positive):
    queries, dim = states.shape
    own_att = attempts.shape[0]
    n_att = own_att * n_blk
    chunk = min(512, queries)
    rows = dim * (dim // 2) // PARTS // LANES
    plan = stage_plan(n_grp, n_blk, rows)
    copies = 2 * (n_blk - 1) + 2 * PARTS
    bf16, f32 = jnp.bfloat16, jnp.float32
    stage_bufs = []
    for stages in plan:
        for axis, stride, size, length, scatter in stages:
            copies += (size - 1) * (2 if scatter else 1)
            stage_bufs.append(pltpu.VMEM((length, LANES), bf16))
            if scatter:
                stage_bufs.append(pltpu.VMEM((size - 1, length // size, LANES), bf16))
            else:
                stage_bufs.append(pltpu.VMEM((size, length, LANES), bf16))
    vmem = pl.BlockSpec(memory_space=pltpu.VMEM)
    loss, grad_att, grad_w = pl.pallas_call(
        functools.partial(kernel, n_grp, n_blk, plan, chunk),
        out_shape=(
            jax.ShapeDtypeStruct((1, queries), f32),
            jax.ShapeDtypeStruct((own_att, dim), f32),
            jax.ShapeDtypeStruct((dim, dim), bf16),
        ),
        in_specs=[vmem] * 5,
        out_specs=(vmem,) * 3,
        scratch_shapes=[
            pltpu.VMEM((dim, dim), bf16),
            pltpu.VMEM((dim, queries), bf16),
            pltpu.VMEM((dim, queries), bf16),
            pltpu.VMEM((n_att, queries), bf16),
            pltpu.VMEM((1, queries), f32),
            pltpu.VMEM((n_att, dim), bf16),
            pltpu.VMEM((dim, n_att), bf16),
            pltpu.VMEM((n_att, dim), bf16),
            pltpu.VMEM((n_blk - 1, own_att, dim), bf16),
            pltpu.VMEM((PARTS, rows, LANES), f32),
            pltpu.VMEM((PARTS, rows, LANES), bf16),
            pltpu.VMEM((PARTS, rows, LANES), bf16),
            pltpu.VMEM((2, PARTS, rows, LANES), bf16),
            pltpu.SemaphoreType.DMA((copies,)),
            pltpu.SemaphoreType.DMA((copies,)),
            *stage_bufs,
        ],
        compiler_params=pltpu.CompilerParams(
            collective_id=0, has_side_effects=True, vmem_limit_bytes=48 * 1024 * 1024
        ),
    )(states, query_weight, attempts, attempt_theorem.reshape(1, n_att), positive.reshape(1, queries))
    return loss.reshape(queries), grad_att, grad_w.astype(f32)


def solution(mesh):
    n_grp, n_blk = mesh.shape["grp"], mesh.shape["blk"]
    in_specs = (P(("grp", "blk"), None), P(), P(("grp", "blk"), None), P("grp"), P(("grp", "blk")))
    out_specs = (P(("grp", "blk")), P(("grp", "blk"), None), P())
    return jax.shard_map(
        functools.partial(on_device, n_grp, n_blk),
        mesh=mesh, in_specs=in_specs, out_specs=out_specs, check_vma=False,
    )
```

time: 198 us -> 56.7 us (0.29)
  waiting for transfers between devices: 131 us -> 0 us
  Pallas kernels: 0 us -> 47.5 us
  matrix products: 17.8 us -> 0 us
  between operations: 15.6 us -> 0.65 us
  local copies, waits for them, and re-layouts: 18.1 us -> 6.69 us
  blocking collectives: 7.8 us -> 0 us
  other arithmetic: 5.33 us -> 1.58 us
    psum x1 -> x0, waiting for transfers between devices: 119 us -> none  [on_device(): grad_weight = lax.psum(weight_term, ('grp', 'blk'))]
    pallas_call x0 -> x1, Pallas kernels: none -> 47.5 us  [on_device(): pl.pallas_call(functools.partial(kernel, n_grp, n_blk, plan, chunk), out_...]
    dot_general x5 -> x0, matrix products: 17.8 us -> none  [the longest x1 5.38 us: on_device(): jnp.dot(weights, panel, preferred_element_type=jnp.float32)]
    gather x1 -> x0, local copies, waits for them, and re-layouts: 13.2 us -> none  [on_device(): anchor_lemma_label = jnp.take(attempt_theorem, positive)]
    reduce_scatter x1 -> x0, waiting for transfers between devices: 11.9 us -> none  [on_device(): lax.psum_scatter((lax.dot_general(weights, query_unit, (((0,), (0,)), (()...]
    all_gather x1 -> x0, blocking collectives: 7.8 us -> none  [on_device(): panel = lax.all_gather(candidate_direction, 'blk', axis=0, tiled=True)]
    reduce_sum x2 -> x0, other arithmetic: 2.19 us -> none  [the longest x1 1.16 us: normalized_rows(): jnp.mean(values * values, axis=-1, keepdims=True) + epsilon]
    unnamed x17 -> x12, local copies, waits for them, and re-layouts: 4.92 us -> 6.69 us
  transfers between devices with their start and end apart: 2 -> 0, of which waited for: 2 -> 0; matrix products, arithmetic and copies ran while one was open for 7% -> 0% of each run, Pallas kernels for 0% -> 0%
where the time goes in v1:
time: 56.7 us; the launch traced here: 56.4 us
  Pallas kernels  47.5 us (84%)
  local copies, waits for them, and re-layouts  6.69 us (12%)
  other arithmetic  1.58 us (3%)
  between operations  0.65 us (1%)
    pallas_call x1, Pallas kernels, on_device(): pl.pallas_call(functools.partial(kernel, n_grp, n_blk, plan, chunk), out_...  47.5 us
    unnamed x12, local copies, waits for them, and re-layouts  6.69 us
    convert_element_type x1, other arithmetic, on_device(): return (loss.reshape(queries), grad_att, grad_w.astype(f32))  1.58 us

profile of v1, /device:TPU:1, one launch (start us, length us, event | category | flops | bytes accessed | tf_op | source)
XLA Modules:
  0.0 56.4 jit_solution(183149933685868090)
XLA Ops:
  0.6 0.0 copy-start
  0.6 1.9 %copy-done = bf16[2048,768]{1,0:T(8,128)(2,1)S(1)} copy-done((bf16[2048,768]{1,0:T(8,128)(2,1)S(1)}, bf16[2048,768]{1,0:T(8,128)(2,1)}, u32[]{:S(2)}) %copy-start) | copy-done | bytes 3145752
  2.5 0.0 copy-start.1
  2.5 1.3 %copy-done.1 = bf16[768,768]{1,0:T(8,128)(2,1)S(1)} copy-done((bf16[768,768]{1,0:T(8,128)(2,1)S(1)}, bf16[768,768]{1,0:T(8,128)(2,1)}, u32[]{:S(2)}) %copy-start.1) | copy-done | bytes 1179672
  3.8 0.0 copy-start.2
  3.8 0.9 %copy-done.2 = bf16[64,768]{1,0:T(8,128)(2,1)S(1)} copy-done((bf16[64,768]{1,0:T(8,128)(2,1)S(1)}, bf16[64,768]{1,0:T(8,128)(2,1)}, u32[]{:S(2)}) %copy-start.2) | copy-done | bytes 98328
  4.7 0.0 copy-start.3
  4.7 0.7 %copy-done.3 = s32[2048]{0:T(1024)S(1)} copy-done((s32[2048]{0:T(1024)S(1)}, s32[2048]{0:T(1024)}, u32[]{:S(2)}) %copy-start.3) | copy-done | bytes 8216
  5.4 0.0 copy-start.4
  5.4 0.7 %copy-done.4 = s32[256]{0:T(256)S(1)} copy-done((s32[256]{0:T(256)S(1)}, s32[256]{0:T(256)}, u32[]{:S(2)}) %copy-start.4) | copy-done | bytes 1048
  6.1 47.5 %shard_map.76 = (f32[1,2048]{1,0:T(1,128)S(1)}, f32[64,768]{1,0:T(8,128)S(1)}, bf16[768,768]{1,0:T(8,128)(2,1)S(1)}) custom-call(bf16[2048,768]{1,0:T(8,128)(2,1)S(1)} %copy-done, bf16[768,768]{1,0:T(8,128)(2,1)S(1)} %copy-done.1, bf16[64,768]{1,0:T(8,128)(2,1)S(1)} %copy-done.2, s32[1,256]{1,0:T(1,128)S(1)} %bitcast.5, s32[1,2048]{1,0:T(1,128)S(1)} %bitcast.3), custom_call_target="tpu_custom_call" | custom-call | tf_op jit(solution)/shard_map/pallas_call | solution.py:312
  53.5 1.6 %convert_element_type.3 = f32[768,768]{1,0:T(8,128)} convert(bf16[768,768]{1,0:T(8,128)(2,1)S(1)} %get-tuple-element.8) | non-fusion elementwise | flops 589824 | bytes 3538944 | tf_op jit(solution)/shard_map/convert_element_type | solution.py:343
  55.1 0.6 %copy.10 = f32[2048]{0:T(1024)} copy(f32[2048]{0:T(1024)S(1)} %bitcast.4) | data formatting | bytes 16384
  55.7 0.7 %copy.11 = f32[64,768]{1,0:T(8,128)} copy(f32[64,768]{1,0:T(8,128)S(1)} %get-tuple-element.13) | data formatting | bytes 393216
Async XLA Ops:
  0.6 1.9 %copy-start = (bf16[2048,768]{1,0:T(8,128)(2,1)S(1)}, bf16[2048,768]{1,0:T(8,128)(2,1)}, u32[]{:S(2)}) copy-start(bf16[2048,768]{1,0:T(8,128)(2,1)} %states.1) | copy-start | bytes 9437188
  2.5 1.3 %copy-start.1 = (bf16[768,768]{1,0:T(8,128)(2,1)S(1)}, bf16[768,768]{1,0:T(8,128)(2,1)}, u32[]{:S(2)}) copy-start(bf16[768,768]{1,0:T(8,128)(2,1)} %weight.1) | copy-start | bytes 3538948
  3.8 0.9 %copy-start.2 = (bf16[64,768]{1,0:T(8,128)(2,1)S(1)}, bf16[64,768]{1,0:T(8,128)(2,1)}, u32[]{:S(2)}) copy-start(bf16[64,768]{1,0:T(8,128)(2,1)} %attempts.1) | copy-start | bytes 294916
  4.7 0.7 %copy-start.3 = (s32[2048]{0:T(1024)S(1)}, s32[2048]{0:T(1024)}, u32[]{:S(2)}) copy-start(s32[2048]{0:T(1024)} %param.9) | copy-start | bytes 24580
  5.4 0.7 %copy-start.4 = (s32[256]{0:T(256)S(1)}, s32[256]{0:T(256)}, u32[]{:S(2)}) copy-start(s32[256]{0:T(256)} %param.8) | copy-start | bytes 3076

commit v2 on v1

--- a/solution.py
+++ b/solution.py
@@ -41,8 +41,9 @@
 
 def kernel(
     n_grp, n_blk, plan, chunk,
-    states, weight, attempts, theorem, positive,
+    states_hbm, weight_hbm, attempts_hbm, theorem_hbm, positive_hbm,
     loss, grad_att, grad_w,
+    states, weight, attempts, theorem, positive, load_sems,
     weight_t, unit_t, gproj_t, w_all, inv_rms, panel, panel_t,
     ga_stage, ga_recv, acc, core_send, core_recv, res, send_sems, recv_sems, *stage_bufs,
 ):
@@ -80,6 +81,26 @@
         started.append(copy)
         return copy
 
+    def load(src, dst, n):
+        return pltpu.make_async_copy(src, dst, load_sems.at[n])
+
+    def load_states(step):
+        rows = pl.ds(pl.multiple_of(step * chunk, chunk), chunk)
+        return load(states_hbm.at[rows], states.at[rows], 4 + step)
+
+    loads = [
+        load(attempts_hbm, attempts, 0),
+        load(weight_hbm, weight, 1),
+        load(theorem_hbm, theorem, 2),
+        load(positive_hbm, positive, 3),
+    ]
+    loads[0].start()
+    loads[1].start()
+    for step in range(queries // chunk):
+        load_states(step).start()
+    loads[2].start()
+    loads[3].start()
+
     greeted = [("blk", 1, n_blk), ("grp", 1, 2), ("grp", 2, n_grp // 2)]
     barrier = pltpu.get_barrier_semaphore()
     count = 0
@@ -90,6 +111,7 @@
             )
             count += 1
 
+    loads[0].wait()
     att = attempts[...].astype(jnp.float32)
     att_r = lax.rsqrt(jnp.mean(att * att, axis=1, keepdims=True) + epsilon)
     att_unit = att * att_r
@@ -101,9 +123,11 @@
         for k in range(1, n_blk)
     ]
 
+    loads[1].wait()
     weight_t[...] = weight[...].T
 
     def project(step, carry):
+        load_states(step).wait()
         cols = pl.ds(pl.multiple_of(step * chunk, chunk), chunk)
         proj = lax.dot_general(
             weight_t[...], states[cols, :], NT, preferred_element_type=jnp.float32
@@ -117,6 +141,8 @@
 
     for copy in gathers:
         copy.wait_recv()
+    loads[2].wait()
+    loads[3].wait()
     panel_t[...] = panel[...].T
     theorem_col = jnp.broadcast_to(theorem[...].astype(jnp.float32), (8, n_att)).T[:, 0:1]
 
@@ -290,6 +316,24 @@
         copy.wait_send()
 
 
+def write_out(loss, grad_att, grad_w, loss_hbm, grad_att_hbm, grad_w_hbm, wide, sems):
+    copies = [
+        pltpu.make_async_copy(loss, loss_hbm, sems.at[0]),
+        pltpu.make_async_copy(grad_att, grad_att_hbm, sems.at[1]),
+    ]
+    for copy in copies:
+        copy.start()
+    step = wide.shape[0] // PARTS
+    for part in range(PARTS):
+        rows = pl.ds(part * step, step)
+        wide[rows, :] = grad_w[rows, :].astype(jnp.float32)
+        copy = pltpu.make_async_copy(wide.at[rows], grad_w_hbm.at[rows], sems.at[2 + part])
+        copy.start()
+        copies.append(copy)
+    for copy in copies:
+        copy.wait()
+
+
 def on_device(n_grp, n_blk, states, query_weight, attempts, attempt_theorem, positive):
     queries, dim = states.shape
     own_att = attempts.shape[0]
@@ -309,6 +353,7 @@
             else:
                 stage_bufs.append(pltpu.VMEM((size, length, LANES), bf16))
     vmem = pl.BlockSpec(memory_space=pltpu.VMEM)
+    hbm = pl.BlockSpec(memory_space=pltpu.HBM)
     loss, grad_att, grad_w = pl.pallas_call(
         functools.partial(kernel, n_grp, n_blk, plan, chunk),
         out_shape=(
@@ -316,9 +361,15 @@
             jax.ShapeDtypeStruct((own_att, dim), f32),
             jax.ShapeDtypeStruct((dim, dim), bf16),
         ),
-        in_specs=[vmem] * 5,
+        in_specs=[hbm] * 5,
         out_specs=(vmem,) * 3,
         scratch_shapes=[
+            pltpu.VMEM((queries, dim), bf16),
+            pltpu.VMEM((dim, dim), bf16),
+            pltpu.VMEM((own_att, dim), bf16),
+            pltpu.VMEM((1, n_att), jnp.int32),
+            pltpu.VMEM((1, queries), jnp.int32),
+            pltpu.SemaphoreType.DMA((4 + queries // chunk,)),
             pltpu.VMEM((dim, dim), bf16),
             pltpu.VMEM((dim, queries), bf16),
             pltpu.VMEM((dim, queries), bf16),
@@ -339,8 +390,20 @@
         compiler_params=pltpu.CompilerParams(
             collective_id=0, has_side_effects=True, vmem_limit_bytes=48 * 1024 * 1024
         ),
-    )(states, query_weight, attempts, attempt_theorem.reshape(1, n_att), positive.reshape(1, queries))
-    return loss.reshape(queries), grad_att, grad_w.astype(f32)
+    )(*[pltpu.with_memory_space_constraint(x, pltpu.HBM) for x in (states, query_weight, attempts, attempt_theorem.reshape(1, n_att), positive.reshape(1, queries))])
+    loss, grad_att, grad_w = pl.pallas_call(
+        write_out,
+        out_shape=(
+            jax.ShapeDtypeStruct((1, queries), f32),
+            jax.ShapeDtypeStruct((own_att, dim), f32),
+            jax.ShapeDtypeStruct((dim, dim), f32),
+        ),
+        in_specs=[vmem] * 3,
+        out_specs=(hbm,) * 3,
+        scratch_shapes=[pltpu.VMEM((dim, dim), f32), pltpu.SemaphoreType.DMA((2 + PARTS,))],
+        compiler_params=pltpu.CompilerParams(vmem_limit_bytes=8 * 1024 * 1024),
+    )(loss, grad_att, grad_w)
+    return loss.reshape(queries), grad_att, grad_w
 
 
 def solution(mesh):

time: 56.7 us -> 50.3 us (0.89)
  local copies, waits for them, and re-layouts: 6.69 us -> 0 us
  Pallas kernels: 47.5 us -> 49.5 us
  other arithmetic: 1.58 us -> 0 us
    unnamed x12 -> x0, local copies, waits for them, and re-layouts: 6.69 us -> none
    convert_element_type x1 -> x0, other arithmetic: 1.58 us -> none  [on_device(): return (loss.reshape(queries), grad_att, grad_w.astype(f32))]
    pallas_call x0 -> x1, Pallas kernels: none -> 1.51 us  [on_device(): pl.pallas_call(write_out, out_shape=(jax.ShapeDtypeStruct((1, queries), f...]
where the time goes in v2:
time: 50.3 us; the launch traced here: 50.2 us
  Pallas kernels  49.5 us (98%)
  between operations  0.64 us (1%)
    pallas_call x1, Pallas kernels, on_device(): pl.pallas_call(functools.partial(kernel, n_grp, n_blk, plan, chunk), out_...  48 us
    pallas_call x1, Pallas kernels, on_device(): pl.pallas_call(write_out, out_shape=(jax.ShapeDtypeStruct((1, queries), f...  1.51 us

profile of v2, /device:TPU:1, one launch (start us, length us, event | category | flops | bytes accessed | tf_op | source)
XLA Modules:
  0.0 50.2 jit_solution(14882081675985157018)
XLA Ops:
  0.6 48.0 %shard_map.76 = (f32[1,2048]{1,0:T(1,128)S(1)}, f32[64,768]{1,0:T(8,128)S(1)}, bf16[768,768]{1,0:T(8,128)(2,1)S(1)}) custom-call(bf16[2048,768]{1,0:T(8,128)(2,1)} %states_hbm.1, bf16[768,768]{1,0:T(8,128)(2,1)} %weight_hbm.1, bf16[64,768]{1,0:T(8,128)(2,1)} %attempts_hbm.1, s32[1,256]{1,0:T(1,128)} %bitcast.4, s32[1,2048]{1,0:T(1,128)} %bitcast.3), custom_call_target="tpu_custom_call" | custom-call | tf_op jit(solution)/shard_map/pallas_call | solution.py:357
  48.6 1.5 %shard_map.77 = (f32[1,2048]{1,0:T(1,128)}, f32[64,768]{1,0:T(8,128)}, f32[768,768]{1,0:T(8,128)}) custom-call(f32[1,2048]{1,0:T(1,128)S(1)} %get-tuple-element.9.loss, f32[64,768]{1,0:T(8,128)S(1)} %get-tuple-element.10.grad_att, bf16[768,768]{1,0:T(8,128)(2,1)S(1)} %get-tuple-element.11.grad_w), custom_call_target="tpu_custom_call" | custom-call | tf_op jit(solution)/shard_map/pallas_call | solution.py:394

commit v3 on v2

v3 whole, which is shorter than its diff:
```python
import functools

import jax
import jax.numpy as jnp
from jax import lax
from jax.experimental import pallas as pl
from jax.experimental.pallas import tpu as pltpu
from jax.sharding import PartitionSpec as P

logit_sharpness = 0.07
epsilon = 1e-06
MESH = pl.DeviceIdType.MESH
PARTS = 3
LANES = 128
TILE = 16
NT = (((1,), (1,)), ((), ()))


def stage_plan(n_grp, n_blk, units):
    along_x = ("blk", 2, n_blk // 2)
    along_y = ("grp", 1, 2)
    along_z = ("grp", 2, n_grp // 2)
    xyz, yxz, zxy = (along_x, along_y, along_z), (along_y, along_x, along_z), (along_z, along_x, along_y)
    pieces = []
    split = (((zxy, 1), (xyz, 1), (yxz, 1)), ((xyz, 2), (yxz, 1)), ((xyz, 1), (yxz, 2)))
    for block, row in enumerate(split):
        first = 0
        for order, count in row:
            rows = length = count * units
            stages = []
            for axis, stride, size in order:
                if size == 1:
                    continue
                scatter = length % (size * TILE) == 0
                stages.append((axis, stride, size, length, scatter))
                if scatter:
                    length //= size
            pieces.append((block, first, rows, stages))
            first += rows
    return pieces


def kernel(
    n_grp, n_blk, plan, chunk,
    states_hbm, weight_hbm, attempts_hbm, theorem_hbm, positive_hbm,
    loss, grad_att, res,
    states, weight, attempts, theorem, positive, load_sems,
    weight_t, unit_t, gproj_t, w_all, inv_rms, along_all, panel, panel_t,
    ga_stage, ga_core, ga_sum, ga_recv, acc, core_send, core_recv, send_sems, recv_sems, *stage_bufs,
):
    queries, dim = states.shape
    own_att = attempts.shape[0]
    n_att = own_att * n_blk
    half = dim // 2
    width = dim // PARTS
    multiplier = 1.0 / (logit_sharpness * dim)
    grp = lax.axis_index("grp")
    blk = lax.axis_index("blk")
    core = lax.rem(blk, 2)
    sibling = blk + 1 - 2 * core
    used = [0]
    started = []

    def member(axis, stride, size):
        index = grp if axis == "grp" else blk
        return lax.rem(index // stride, size)

    def partner(axis, stride, size, k):
        index = grp if axis == "grp" else blk
        here = lax.rem(index // stride, size)
        there = lax.rem(here + k, size)
        return {axis: index + (there - here) * stride}, there

    def send(src, dst, device):
        n = used[0]
        used[0] += 1
        copy = pltpu.make_async_remote_copy(
            src_ref=src, dst_ref=dst, send_sem=send_sems.at[n], recv_sem=recv_sems.at[n],
            device_id=device, device_id_type=MESH,
        )
        copy.start()
        started.append(copy)
        return copy

    def load(src, dst, n):
        return pltpu.make_async_copy(src, dst, load_sems.at[n])

    def load_states(step):
        rows = pl.ds(pl.multiple_of(step * chunk, chunk), chunk)
        return load(states_hbm.at[rows], states.at[rows], 4 + step)

    loads = [
        load(attempts_hbm, attempts, 0),
        load(weight_hbm, weight, 1),
        load(theorem_hbm, theorem, 2),
        load(positive_hbm, positive, 3),
    ]
    loads[0].start()
    loads[1].start()
    for step in range(queries // chunk):
        load_states(step).start()
    loads[2].start()
    loads[3].start()

    greeted = [("blk", 1, n_blk), ("grp", 1, 2), ("grp", 2, n_grp // 2)]
    barrier = pltpu.get_barrier_semaphore()
    count = 0
    for axis, stride, size in greeted:
        for k in range(1, size):
            pl.semaphore_signal(
                barrier, inc=1, device_id=partner(axis, stride, size, k)[0], device_id_type=MESH
            )
            count += 1

    loads[0].wait()
    att = attempts[...].astype(jnp.float32)
    att_r = lax.rsqrt(jnp.mean(att * att, axis=1, keepdims=True) + epsilon)
    att_unit = att * att_r
    own_rows = pl.ds(pl.multiple_of(blk * own_att, own_att), own_att)
    panel[own_rows, :] = att_unit.astype(jnp.bfloat16)
    pl.semaphore_wait(barrier, count)
    across = [
        send(panel.at[own_rows], panel.at[own_rows], partner("blk", 2, n_blk // 2, k)[0])
        for k in range(1, n_blk // 2)
    ]
    to_sibling = [send(panel.at[own_rows], panel.at[own_rows], {"blk": sibling})]

    loads[1].wait()
    weight_t[...] = weight[...].T

    def project(step, carry):
        load_states(step).wait()
        cols = pl.ds(pl.multiple_of(step * chunk, chunk), chunk)
        proj = lax.dot_general(
            weight_t[...], states[cols, :], NT, preferred_element_type=jnp.float32
        )
        r = lax.rsqrt(jnp.sum(proj * proj, axis=0, keepdims=True) * (1.0 / dim) + epsilon)
        inv_rms[:, cols] = r
        unit_t[:, cols] = (proj * r).astype(jnp.bfloat16)
        return carry

    steps = queries // chunk
    lax.fori_loop(0, steps // 2, project, 0)
    for k, copy in enumerate(across):
        copy.wait_recv()
        source = lax.rem(blk // 2 + n_blk // 2 - (k + 1), n_blk // 2) * 2 + core
        rows = pl.ds(pl.multiple_of(source * own_att, own_att), own_att)
        to_sibling.append(send(panel.at[rows], panel.at[rows], {"blk": sibling}))
    lax.fori_loop(steps // 2, steps, project, 0)

    for copy in to_sibling:
        copy.wait_recv()
    loads[2].wait()
    loads[3].wait()
    panel_t[...] = panel[...].T
    theorem_col = jnp.broadcast_to(theorem[...].astype(jnp.float32), (8, n_att)).T[:, 0:1]

    def contrast(step, carry):
        cols = pl.ds(pl.multiple_of(step * chunk, chunk), chunk)
        unit = unit_t[:, cols]
        scores = jnp.dot(panel[...], unit, preferred_element_type=jnp.float32) * multiplier
        chosen = lax.broadcasted_iota(jnp.int32, scores.shape, 0) == positive[:, cols]
        label = jnp.sum(jnp.where(chosen, theorem_col, 0.0), axis=0, keepdims=True)
        expo = jnp.where(theorem_col == label, jnp.exp(scores), 0.0)
        total = jnp.sum(expo, axis=0, keepdims=True)
        pos_score = jnp.sum(jnp.where(chosen, scores, 0.0), axis=0, keepdims=True)
        loss[:, cols] = jnp.log(total) - pos_score
        w = (expo * (1.0 / total) - jnp.where(chosen, 1.0, 0.0)).astype(jnp.bfloat16)
        w_all[:, cols] = w
        along = jnp.sum(w.astype(jnp.float32) * scores, axis=0, keepdims=True) * (1.0 / dim)
        along_all[:, cols] = along * inv_rms[:, cols]
        return carry

    lax.fori_loop(0, steps, contrast, 0)

    begin = [first for block, first, rows, stages in plan]
    pending = [None] * len(plan)
    bufs, n = [], 0
    for block, first, rows, stages in plan:
        bufs.append([(stage_bufs[n + 2 * j], stage_bufs[n + 2 * j + 1]) for j in range(len(stages))])
        n += 2 * len(stages)

    def start_stage(piece, j):
        block = plan[piece][0]
        axis, stride, size, length, scatter = plan[piece][3][j]
        stage, recv = bufs[piece][j]
        here = member(axis, stride, size)
        rows = pl.ds(pl.multiple_of(begin[piece], TILE), length)
        stage[...] = acc[block, rows, :].astype(jnp.bfloat16)
        pending[piece] = []
        for k in range(1, size):
            device, there = partner(axis, stride, size, k)
            if scatter:
                part = length // size
                src = stage.at[pl.ds(pl.multiple_of(there * part, TILE), part)]
                pending[piece].append(send(src, recv.at[k - 1], device))
            else:
                pending[piece].append(send(stage, recv.at[here], device))

    def finish_stage(piece, j):
        block = plan[piece][0]
        axis, stride, size, length, scatter = plan[piece][3][j]
        stage, recv = bufs[piece][j]
        here = member(axis, stride, size)
        for copy in pending[piece]:
            copy.wait_recv()
        if scatter:
            part = length // size
            begin[piece] = begin[piece] + here * part
            rows = pl.ds(pl.multiple_of(begin[piece], TILE), part)
            total = acc[block, rows, :]
            for k in range(size - 1):
                total = total + recv[k].astype(jnp.float32)
        else:
            rows = pl.ds(pl.multiple_of(begin[piece], TILE), length)
            recv[here] = stage[...]
            total = recv[0].astype(jnp.float32)
            for k in range(1, size):
                total = total + recv[k].astype(jnp.float32)
        if j + 1 < len(plan[piece][3]):
            acc[block, rows, :] = total
        else:
            res[core, block, rows, :] = total.astype(jnp.bfloat16)

    def start_back(piece, j):
        block = plan[piece][0]
        axis, stride, size, length, scatter = plan[piece][3][j]
        part = length // size
        rows = pl.ds(pl.multiple_of(begin[piece], TILE), part)
        spot = res.at[core, block, rows]
        pending[piece] = [
            send(spot, spot, partner(axis, stride, size, k)[0]) for k in range(1, size)
        ]
        begin[piece] = begin[piece] - member(axis, stride, size) * part

    def steps_of(piece):
        block, first, rows, stages = plan[piece]
        start_stage(piece, 0)
        yield
        for j in range(len(stages)):
            finish_stage(piece, j)
            if j + 1 < len(stages):
                start_stage(piece, j + 1)
                yield
        for j in reversed(range(len(stages))):
            if stages[j][4]:
                start_back(piece, j)
                yield
                for copy in pending[piece]:
                    copy.wait_recv()
        spot = res.at[core, block, pl.ds(first, rows)]
        pending[piece] = [send(spot, spot, {"blk": sibling})]
        yield
        pending[piece][0].wait_recv()

    runs = [steps_of(piece) for piece in range(len(plan))]

    def advance(block):
        more = False
        for piece in range(len(plan)):
            if plan[piece][0] == block:
                more = next(runs[piece], "end") != "end" or more
        return more

    slabs = width // LANES
    subs = half // LANES
    core_copies = []

    def grad_proj_third(block):
        rows = slice(block * width, (block + 1) * width)
        g = jnp.dot(panel_t[rows, :], w_all[...], preferred_element_type=jnp.float32)
        gproj_t[rows, :] = (
            g * (inv_rms[...] * multiplier) - unit_t[rows, :].astype(jnp.float32) * along_all[...]
        ).astype(jnp.bfloat16)

    def weight_third(block):
        rows = slice(block * width, (block + 1) * width)
        for which, keep in ((1 - core, False), (core, True)):
            cols = pl.ds(pl.multiple_of(which * half, half), half)
            tile = jnp.dot(
                gproj_t[rows, :], states[:, cols], preferred_element_type=jnp.float32
            ).T
            for u in range(subs):
                for e in range(slabs):
                    at = slice((u * slabs + e) * LANES, (u * slabs + e + 1) * LANES)
                    value = tile[u * LANES:(u + 1) * LANES, e * LANES:(e + 1) * LANES]
                    if keep:
                        acc[block, at, :] = value
                    else:
                        core_send[block, at, :] = value.astype(jnp.bfloat16)
            if not keep:
                core_copies.append(send(core_send.at[block], core_recv.at[block], {"blk": sibling}))

    def add_sibling(block):
        core_copies[block].wait_recv()
        acc[block] += core_recv[block].astype(jnp.float32)

    for block in range(PARTS):
        grad_proj_third(block)
        if block >= 1:
            add_sibling(block - 1)
            advance(block - 1)
        weight_third(block)

    advance(0)
    ga = lax.dot_general(unit_t[...], w_all[...], NT, preferred_element_type=jnp.float32)
    ga = (ga * multiplier).T.astype(jnp.bfloat16)
    for owner in range(n_blk):
        ga_stage[owner % 2, owner // 2] = ga[owner * own_att:(owner + 1) * own_att, :]
    ga_copy = send(ga_stage.at[1 - core], ga_core, {"blk": sibling})
    add_sibling(PARTS - 1)
    advance(PARTS - 1)
    advance(1)
    advance(0)
    advance(2)
    advance(1)
    advance(0)

    ga_copy.wait_recv()
    ga_sum[...] = (
        ga_stage[core].astype(jnp.float32) + ga_core[...].astype(jnp.float32)
    ).astype(jnp.bfloat16)
    ga_copies = []
    for k in range(1, n_blk // 2):
        device, owner = partner("blk", 2, n_blk // 2, k)
        ga_copies.append(send(ga_sum.at[owner], ga_recv.at[k - 1], device))

    advance(2)
    advance(1)
    advance(0)
    advance(2)
    advance(1)
    advance(0)
    for copy in ga_copies:
        copy.wait_recv()
    ga = ga_stage[core, blk // 2].astype(jnp.float32) + ga_core[blk // 2].astype(jnp.float32)
    for k in range(n_blk // 2 - 1):
        ga = ga + ga_recv[k].astype(jnp.float32)
    att = attempts[...].astype(jnp.float32)
    att_r = lax.rsqrt(jnp.mean(att * att, axis=1, keepdims=True) + epsilon)
    att_unit = att * att_r
    grad_att[...] = att_r * (ga - att_unit * jnp.mean(ga * att_unit, axis=1, keepdims=True))

    more = True
    while more:
        more = any([advance(block) for block in (2, 1, 0)])
    for copy in started:
        copy.wait_send()


def write_out(loss, grad_att, res, loss_hbm, grad_att_hbm, grad_w_hbm, wide, sems):
    copies = [
        pltpu.make_async_copy(loss, loss_hbm, sems.at[0]),
        pltpu.make_async_copy(grad_att, grad_att_hbm, sems.at[1]),
    ]
    for copy in copies:
        copy.start()
    dim = wide.shape[0]
    half, width = dim // 2, dim // PARTS
    slabs, subs = width // LANES, half // LANES
    for which in range(2):
        for u in range(subs):
            row = which * half + u * LANES
            for block in range(PARTS):
                for e in range(slabs):
                    at = (u * slabs + e) * LANES
                    col = block * width + e * LANES
                    wide[row:row + LANES, col:col + LANES] = (
                        res[which, block, at:at + LANES, :].astype(jnp.float32)
                    )
            rows = pl.ds(row, LANES)
            copy = pltpu.make_async_copy(
                wide.at[rows], grad_w_hbm.at[rows], sems.at[2 + which * subs + u]
            )
            copy.start()
            copies.append(copy)
    for copy in copies:
        copy.wait()


def on_device(n_grp, n_blk, states, query_weight, attempts, attempt_theorem, positive):
    queries, dim = states.shape
    own_att = attempts.shape[0]
    n_att = own_att * n_blk
    chunk = min(512, queries)
    rows = dim * (dim // 2) // PARTS // LANES
    plan = stage_plan(n_grp, n_blk, rows // 3)
    copies = 2 * n_blk + 2 * PARTS + len(plan)
    bf16, f32 = jnp.bfloat16, jnp.float32
    stage_bufs = []
    for block, first, count, stages in plan:
        for axis, stride, size, length, scatter in stages:
            copies += (size - 1) * (2 if scatter else 1)
            stage_bufs.append(pltpu.VMEM((length, LANES), bf16))
            if scatter:
                stage_bufs.append(pltpu.VMEM((size - 1, length // size, LANES), bf16))
            else:
                stage_bufs.append(pltpu.VMEM((size, length, LANES), bf16))
    vmem = pl.BlockSpec(memory_space=pltpu.VMEM)
    hbm = pl.BlockSpec(memory_space=pltpu.HBM)
    loss, grad_att, res = pl.pallas_call(
        functools.partial(kernel, n_grp, n_blk, plan, chunk),
        out_shape=(
            jax.ShapeDtypeStruct((1, queries), f32),
            jax.ShapeDtypeStruct((own_att, dim), f32),
            jax.ShapeDtypeStruct((2, PARTS, rows, LANES), bf16),
        ),
        in_specs=[hbm] * 5,
        out_specs=(vmem,) * 3,
        scratch_shapes=[
            pltpu.VMEM((queries, dim), bf16),
            pltpu.VMEM((dim, dim), bf16),
            pltpu.VMEM((own_att, dim), bf16),
            pltpu.VMEM((1, n_att), jnp.int32),
            pltpu.VMEM((1, queries), jnp.int32),
            pltpu.SemaphoreType.DMA((4 + queries // chunk,)),
            pltpu.VMEM((dim, dim), bf16),
            pltpu.VMEM((dim, queries), bf16),
            pltpu.VMEM((dim, queries), bf16),
            pltpu.VMEM((n_att, queries), bf16),
            pltpu.VMEM((1, queries), f32),
            pltpu.VMEM((1, queries), f32),
            pltpu.VMEM((n_att, dim), bf16),
            pltpu.VMEM((dim, n_att), bf16),
            pltpu.VMEM((2, n_blk // 2, own_att, dim), bf16),
            pltpu.VMEM((n_blk // 2, own_att, dim), bf16),
            pltpu.VMEM((n_blk // 2, own_att, dim), bf16),
            pltpu.VMEM((max(n_blk // 2 - 1, 1), own_att, dim), bf16),
            pltpu.VMEM((PARTS, rows, LANES), f32),
            pltpu.VMEM((PARTS, rows, LANES), bf16),
            pltpu.VMEM((PARTS, rows, LANES), bf16),
            pltpu.SemaphoreType.DMA((copies,)),
            pltpu.SemaphoreType.DMA((copies,)),
            *stage_bufs,
        ],
        compiler_params=pltpu.CompilerParams(
            collective_id=0, has_side_effects=True, vmem_limit_bytes=48 * 1024 * 1024
        ),
    )(*[pltpu.with_memory_space_constraint(x, pltpu.HBM) for x in (states, query_weight, attempts, attempt_theorem.reshape(1, n_att), positive.reshape(1, queries))])
    loss, grad_att, grad_w = pl.pallas_call(
        write_out,
        out_shape=(
            jax.ShapeDtypeStruct((1, queries), f32),
            jax.ShapeDtypeStruct((own_att, dim), f32),
            jax.ShapeDtypeStruct((dim, dim), f32),
        ),
        in_specs=[vmem] * 3,
        out_specs=(hbm,) * 3,
        scratch_shapes=[pltpu.VMEM((dim, dim), f32), pltpu.SemaphoreType.DMA((2 + dim // LANES,))],
        compiler_params=pltpu.CompilerParams(vmem_limit_bytes=8 * 1024 * 1024),
    )(loss, grad_att, res)
    return loss.reshape(queries), grad_att, grad_w


def solution(mesh):
    n_grp, n_blk = mesh.shape["grp"], mesh.shape["blk"]
    in_specs = (P(("grp", "blk"), None), P(), P(("grp", "blk"), None), P("grp"), P(("grp", "blk")))
    out_specs = (P(("grp", "blk")), P(("grp", "blk"), None), P())
    return jax.shard_map(
        functools.partial(on_device, n_grp, n_blk),
        mesh=mesh, in_specs=in_specs, out_specs=out_specs, check_vma=False,
    )
```

time: 50.3 us -> 47.3 us (0.940)
  Pallas kernels: 49.5 us -> 46.5 us
    pallas_call x1, Pallas kernels: 48 us -> 45 us  [on_device(): pl.pallas_call(functools.partial(kernel, n_grp, n_blk, plan, chunk), out_...]
where the time goes in v3:
time: 47.3 us; the launch traced here: 47.1 us
  Pallas kernels  46.5 us (98%)
  between operations  0.64 us (1%)
    pallas_call x1, Pallas kernels, on_device(): pl.pallas_call(functools.partial(kernel, n_grp, n_blk, plan, chunk), out_...  45 us
    pallas_call x1, Pallas kernels, on_device(): pl.pallas_call(write_out, out_shape=(jax.ShapeDtypeStruct((1, queries), f...  1.53 us

profile of v3, /device:TPU:1, one launch (start us, length us, event | category | flops | bytes accessed | tf_op | source)
XLA Modules:
  0.0 47.1 jit_solution(7008991828697674590)
XLA Ops:
  0.6 45.0 %shard_map.76 = (f32[1,2048]{1,0:T(1,128)S(1)}, f32[64,768]{1,0:T(8,128)S(1)}, bf16[2,3,768,128]{3,2,1,0:T(8,128)(2,1)S(1)}) custom-call(bf16[2048,768]{1,0:T(8,128)(2,1)} %states_hbm.1, bf16[768,768]{1,0:T(8,128)(2,1)} %weight_hbm.1, bf16[64,768]{1,0:T(8,128)(2,1)} %attempts_hbm.1, s32[1,256]{1,0:T(1,128)} %bitcast.4, s32[1,2048]{1,0:T(1,128)} %bitcast.3), custom_call_target="tpu_custom_call" | custom-call | tf_op jit(solution)/shard_map/pallas_call | solution.py:401
  45.6 1.5 %shard_map.77 = (f32[1,2048]{1,0:T(1,128)}, f32[64,768]{1,0:T(8,128)}, f32[768,768]{1,0:T(8,128)}) custom-call(f32[1,2048]{1,0:T(1,128)S(1)} %get-tuple-element.9.loss, f32[64,768]{1,0:T(8,128)S(1)} %get-tuple-element.10.grad_att, bf16[2,3,768,128]{3,2,1,0:T(8,128)(2,1)S(1)} %get-tuple-element.11.res), custom_call_target="tpu_custom_call" | custom-call | tf_op jit(solution)/shard_map/pallas_call | solution.py:440

commit v4 on v3

--- a/solution.py
+++ b/solution.py
@@ -45,7 +45,7 @@
     states_hbm, weight_hbm, attempts_hbm, theorem_hbm, positive_hbm,
     loss, grad_att, res,
     states, weight, attempts, theorem, positive, load_sems,
-    weight_t, unit_t, gproj_t, w_all, inv_rms, along_all, panel, panel_t,
+    weight_t, unit_t, gproj_t, w_all, inv_rms, panel, panel_t,
     ga_stage, ga_core, ga_sum, ga_recv, acc, core_send, core_recv, send_sems, recv_sems, *stage_bufs,
 ):
     queries, dim = states.shape
@@ -128,25 +128,26 @@
     loads[1].wait()
     weight_t[...] = weight[...].T
 
-    def project(step, carry):
+    def project(step):
         load_states(step).wait()
-        cols = pl.ds(pl.multiple_of(step * chunk, chunk), chunk)
+        cols = pl.ds(step * chunk, chunk)
         proj = lax.dot_general(
             weight_t[...], states[cols, :], NT, preferred_element_type=jnp.float32
         )
         r = lax.rsqrt(jnp.sum(proj * proj, axis=0, keepdims=True) * (1.0 / dim) + epsilon)
         inv_rms[:, cols] = r
         unit_t[:, cols] = (proj * r).astype(jnp.bfloat16)
-        return carry
 
     steps = queries // chunk
-    lax.fori_loop(0, steps // 2, project, 0)
+    for step in range(steps // 2):
+        project(step)
     for k, copy in enumerate(across):
         copy.wait_recv()
         source = lax.rem(blk // 2 + n_blk // 2 - (k + 1), n_blk // 2) * 2 + core
         rows = pl.ds(pl.multiple_of(source * own_att, own_att), own_att)
         to_sibling.append(send(panel.at[rows], panel.at[rows], {"blk": sibling}))
-    lax.fori_loop(steps // 2, steps, project, 0)
+    for step in range(steps // 2, steps):
+        project(step)
 
     for copy in to_sibling:
         copy.wait_recv()
@@ -155,8 +156,8 @@
     panel_t[...] = panel[...].T
     theorem_col = jnp.broadcast_to(theorem[...].astype(jnp.float32), (8, n_att)).T[:, 0:1]
 
-    def contrast(step, carry):
-        cols = pl.ds(pl.multiple_of(step * chunk, chunk), chunk)
+    def contrast(step):
+        cols = pl.ds(step * chunk, chunk)
         unit = unit_t[:, cols]
         scores = jnp.dot(panel[...], unit, preferred_element_type=jnp.float32) * multiplier
         chosen = lax.broadcasted_iota(jnp.int32, scores.shape, 0) == positive[:, cols]
@@ -168,10 +169,14 @@
         w = (expo * (1.0 / total) - jnp.where(chosen, 1.0, 0.0)).astype(jnp.bfloat16)
         w_all[:, cols] = w
         along = jnp.sum(w.astype(jnp.float32) * scores, axis=0, keepdims=True) * (1.0 / dim)
-        along_all[:, cols] = along * inv_rms[:, cols]
-        return carry
-
-    lax.fori_loop(0, steps, contrast, 0)
+        r = inv_rms[:, cols]
+        g = jnp.dot(panel_t[...], w, preferred_element_type=jnp.float32)
+        gproj_t[:, cols] = (
+            g * (r * multiplier) - unit.astype(jnp.float32) * (r * along)
+        ).astype(jnp.bfloat16)
+
+    for step in range(steps):
+        contrast(step)
 
     begin = [first for block, first, rows, stages in plan]
     pending = [None] * len(plan)
@@ -186,7 +191,7 @@
         stage, recv = bufs[piece][j]
         here = member(axis, stride, size)
         rows = pl.ds(pl.multiple_of(begin[piece], TILE), length)
-        stage[...] = acc[block, rows, :].astype(jnp.bfloat16)
+        stage[...] = acc[block, core, rows, :].astype(jnp.bfloat16)
         pending[piece] = []
         for k in range(1, size):
             device, there = partner(axis, stride, size, k)
@@ -208,7 +213,7 @@
             part = length // size
             begin[piece] = begin[piece] + here * part
             rows = pl.ds(pl.multiple_of(begin[piece], TILE), part)
-            total = acc[block, rows, :]
+            total = acc[block, core, rows, :]
             for k in range(size - 1):
                 total = total + recv[k].astype(jnp.float32)
         else:
@@ -218,7 +223,7 @@
             for k in range(1, size):
                 total = total + recv[k].astype(jnp.float32)
         if j + 1 < len(plan[piece][3]):
-            acc[block, rows, :] = total
+            acc[block, core, rows, :] = total
         else:
             res[core, block, rows, :] = total.astype(jnp.bfloat16)
 
@@ -262,45 +267,30 @@
                 more = next(runs[piece], "end") != "end" or more
         return more
 
-    slabs = width // LANES
-    subs = half // LANES
+    slabs = half // LANES
     core_copies = []
 
-    def grad_proj_third(block):
-        rows = slice(block * width, (block + 1) * width)
-        g = jnp.dot(panel_t[rows, :], w_all[...], preferred_element_type=jnp.float32)
-        gproj_t[rows, :] = (
-            g * (inv_rms[...] * multiplier) - unit_t[rows, :].astype(jnp.float32) * along_all[...]
-        ).astype(jnp.bfloat16)
-
     def weight_third(block):
-        rows = slice(block * width, (block + 1) * width)
-        for which, keep in ((1 - core, False), (core, True)):
-            cols = pl.ds(pl.multiple_of(which * half, half), half)
-            tile = jnp.dot(
-                gproj_t[rows, :], states[:, cols], preferred_element_type=jnp.float32
-            ).T
-            for u in range(subs):
-                for e in range(slabs):
-                    at = slice((u * slabs + e) * LANES, (u * slabs + e + 1) * LANES)
-                    value = tile[u * LANES:(u + 1) * LANES, e * LANES:(e + 1) * LANES]
-                    if keep:
-                        acc[block, at, :] = value
-                    else:
-                        core_send[block, at, :] = value.astype(jnp.bfloat16)
-            if not keep:
-                core_copies.append(send(core_send.at[block], core_recv.at[block], {"blk": sibling}))
+        tile = jnp.dot(
+            gproj_t[...], states[:, block * width:(block + 1) * width],
+            preferred_element_type=jnp.float32,
+        ).T
+        for which in range(2):
+            for e in range(slabs):
+                col = which * half + e * LANES
+                acc[block, which, e * width:(e + 1) * width, :] = tile[:, col:col + LANES]
+        core_send[block] = acc[block, 1 - core].astype(jnp.bfloat16)
+        core_copies.append(send(core_send.at[block], core_recv.at[block], {"blk": sibling}))
 
     def add_sibling(block):
         core_copies[block].wait_recv()
-        acc[block] += core_recv[block].astype(jnp.float32)
+        acc[block, core] += core_recv[block].astype(jnp.float32)
 
     for block in range(PARTS):
-        grad_proj_third(block)
+        weight_third(block)
         if block >= 1:
             add_sibling(block - 1)
             advance(block - 1)
-        weight_third(block)
 
     advance(0)
     ga = lax.dot_general(unit_t[...], w_all[...], NT, preferred_element_type=jnp.float32)
@@ -357,23 +347,18 @@
         copy.start()
     dim = wide.shape[0]
     half, width = dim // 2, dim // PARTS
-    slabs, subs = width // LANES, half // LANES
-    for which in range(2):
-        for u in range(subs):
-            row = which * half + u * LANES
-            for block in range(PARTS):
-                for e in range(slabs):
-                    at = (u * slabs + e) * LANES
-                    col = block * width + e * LANES
-                    wide[row:row + LANES, col:col + LANES] = (
-                        res[which, block, at:at + LANES, :].astype(jnp.float32)
-                    )
-            rows = pl.ds(row, LANES)
-            copy = pltpu.make_async_copy(
-                wide.at[rows], grad_w_hbm.at[rows], sems.at[2 + which * subs + u]
-            )
-            copy.start()
-            copies.append(copy)
+    slabs = half // LANES
+    for block in range(PARTS):
+        rows = pl.ds(block * width, width)
+        for which in range(2):
+            for e in range(slabs):
+                col = which * half + e * LANES
+                wide[rows, col:col + LANES] = (
+                    res[which, block, e * width:(e + 1) * width, :].astype(jnp.float32)
+                )
+        copy = pltpu.make_async_copy(wide.at[rows], grad_w_hbm.at[rows], sems.at[2 + block])
+        copy.start()
+        copies.append(copy)
     for copy in copies:
         copy.wait()
 
@@ -419,14 +404,13 @@
             pltpu.VMEM((dim, queries), bf16),
             pltpu.VMEM((n_att, queries), bf16),
             pltpu.VMEM((1, queries), f32),
-            pltpu.VMEM((1, queries), f32),
             pltpu.VMEM((n_att, dim), bf16),
             pltpu.VMEM((dim, n_att), bf16),
             pltpu.VMEM((2, n_blk // 2, own_att, dim), bf16),
             pltpu.VMEM((n_blk // 2, own_att, dim), bf16),
             pltpu.VMEM((n_blk // 2, own_att, dim), bf16),
             pltpu.VMEM((max(n_blk // 2 - 1, 1), own_att, dim), bf16),
-            pltpu.VMEM((PARTS, rows, LANES), f32),
+            pltpu.VMEM((PARTS, 2, rows, LANES), f32),
             pltpu.VMEM((PARTS, rows, LANES), bf16),
             pltpu.VMEM((PARTS, rows, LANES), bf16),
             pltpu.SemaphoreType.DMA((copies,)),
@@ -446,7 +430,7 @@
         ),
         in_specs=[vmem] * 3,
         out_specs=(hbm,) * 3,
-        scratch_shapes=[pltpu.VMEM((dim, dim), f32), pltpu.SemaphoreType.DMA((2 + dim // LANES,))],
+        scratch_shapes=[pltpu.VMEM((dim, dim), f32), pltpu.SemaphoreType.DMA((2 + PARTS,))],
         compiler_params=pltpu.CompilerParams(vmem_limit_bytes=8 * 1024 * 1024),
     )(loss, grad_att, res)
     return loss.reshape(queries), grad_att, grad_w

time: 47.3 us -> 50.1 us (1.059)
  Pallas kernels: 46.5 us -> 49.3 us
    pallas_call x1, Pallas kernels: 45 us -> 47.8 us  [on_device(): pl.pallas_call(functools.partial(kernel, n_grp, n_blk, plan, chunk), out_...]
where the time goes in v4:
time: 50.1 us; the launch traced here: 49.9 us
  Pallas kernels  49.3 us (98%)
  between operations  0.64 us (1%)
    pallas_call x1, Pallas kernels, on_device(): pl.pallas_call(functools.partial(kernel, n_grp, n_blk, plan, chunk), out_...  47.8 us
    pallas_call x1, Pallas kernels, on_device(): pl.pallas_call(write_out, out_shape=(jax.ShapeDtypeStruct((1, queries), f...  1.51 us

profile of v4, /device:TPU:1, one launch (start us, length us, event | category | flops | bytes accessed | tf_op | source)
XLA Modules:
  0.0 49.9 jit_solution(12212284065144546399)
XLA Ops:
  0.6 47.8 %shard_map.76 = (f32[1,2048]{1,0:T(1,128)S(1)}, f32[64,768]{1,0:T(8,128)S(1)}, bf16[2,3,768,128]{3,2,1,0:T(8,128)(2,1)S(1)}) custom-call(bf16[2048,768]{1,0:T(8,128)(2,1)} %states_hbm.1, bf16[768,768]{1,0:T(8,128)(2,1)} %weight_hbm.1, bf16[64,768]{1,0:T(8,128)(2,1)} %attempts_hbm.1, s32[1,256]{1,0:T(1,128)} %bitcast.4, s32[1,2048]{1,0:T(1,128)} %bitcast.3), custom_call_target="tpu_custom_call" | custom-call | tf_op jit(solution)/shard_map/pallas_call | solution.py:386
  48.4 1.5 %shard_map.77 = (f32[1,2048]{1,0:T(1,128)}, f32[64,768]{1,0:T(8,128)}, f32[768,768]{1,0:T(8,128)}) custom-call(f32[1,2048]{1,0:T(1,128)S(1)} %get-tuple-element.9.loss, f32[64,768]{1,0:T(8,128)S(1)} %get-tuple-element.10.grad_att, bf16[2,3,768,128]{3,2,1,0:T(8,128)(2,1)S(1)} %get-tuple-element.11.res), custom_call_target="tpu_custom_call" | custom-call | tf_op jit(solution)/shard_map/pallas_call | solution.py:424

commit v5 on v4

--- a/solution.py
+++ b/solution.py
@@ -128,26 +128,25 @@
     loads[1].wait()
     weight_t[...] = weight[...].T
 
-    def project(step):
+    def project(step, carry):
         load_states(step).wait()
-        cols = pl.ds(step * chunk, chunk)
+        cols = pl.ds(pl.multiple_of(step * chunk, chunk), chunk)
         proj = lax.dot_general(
             weight_t[...], states[cols, :], NT, preferred_element_type=jnp.float32
         )
         r = lax.rsqrt(jnp.sum(proj * proj, axis=0, keepdims=True) * (1.0 / dim) + epsilon)
         inv_rms[:, cols] = r
         unit_t[:, cols] = (proj * r).astype(jnp.bfloat16)
+        return carry
 
     steps = queries // chunk
-    for step in range(steps // 2):
-        project(step)
+    lax.fori_loop(0, steps // 2, project, 0)
     for k, copy in enumerate(across):
         copy.wait_recv()
         source = lax.rem(blk // 2 + n_blk // 2 - (k + 1), n_blk // 2) * 2 + core
         rows = pl.ds(pl.multiple_of(source * own_att, own_att), own_att)
         to_sibling.append(send(panel.at[rows], panel.at[rows], {"blk": sibling}))
-    for step in range(steps // 2, steps):
-        project(step)
+    lax.fori_loop(steps // 2, steps, project, 0)
 
     for copy in to_sibling:
         copy.wait_recv()
@@ -156,8 +155,8 @@
     panel_t[...] = panel[...].T
     theorem_col = jnp.broadcast_to(theorem[...].astype(jnp.float32), (8, n_att)).T[:, 0:1]
 
-    def contrast(step):
-        cols = pl.ds(step * chunk, chunk)
+    def contrast(step, carry):
+        cols = pl.ds(pl.multiple_of(step * chunk, chunk), chunk)
         unit = unit_t[:, cols]
         scores = jnp.dot(panel[...], unit, preferred_element_type=jnp.float32) * multiplier
         chosen = lax.broadcasted_iota(jnp.int32, scores.shape, 0) == positive[:, cols]
@@ -174,9 +173,9 @@
         gproj_t[:, cols] = (
             g * (r * multiplier) - unit.astype(jnp.float32) * (r * along)
         ).astype(jnp.bfloat16)
-
-    for step in range(steps):
-        contrast(step)
+        return carry
+
+    lax.fori_loop(0, steps, contrast, 0)
 
     begin = [first for block, first, rows, stages in plan]
     pending = [None] * len(plan)
@@ -271,14 +270,17 @@
     core_copies = []
 
     def weight_third(block):
-        tile = jnp.dot(
-            gproj_t[...], states[:, block * width:(block + 1) * width],
-            preferred_element_type=jnp.float32,
-        ).T
-        for which in range(2):
+        def one_half(which, carry):
+            rows = pl.ds(pl.multiple_of(which * half, LANES), half)
+            tile = jnp.dot(
+                gproj_t[rows, :], states[:, block * width:(block + 1) * width],
+                preferred_element_type=jnp.float32,
+            ).T
             for e in range(slabs):
-                col = which * half + e * LANES
-                acc[block, which, e * width:(e + 1) * width, :] = tile[:, col:col + LANES]
+                acc[block, which, e * width:(e + 1) * width, :] = tile[:, e * LANES:(e + 1) * LANES]
+            return carry
+
+        lax.fori_loop(0, 2, one_half, 0)
         core_send[block] = acc[block, 1 - core].astype(jnp.bfloat16)
         core_copies.append(send(core_send.at[block], core_recv.at[block], {"blk": sibling}))
 
@@ -293,10 +295,17 @@
             advance(block - 1)
 
     advance(0)
-    ga = lax.dot_general(unit_t[...], w_all[...], NT, preferred_element_type=jnp.float32)
-    ga = (ga * multiplier).T.astype(jnp.bfloat16)
-    for owner in range(n_blk):
-        ga_stage[owner % 2, owner // 2] = ga[owner * own_att:(owner + 1) * own_att, :]
+    def att_third(block, carry):
+        cols = pl.ds(pl.multiple_of(block * width, LANES), width)
+        ga = lax.dot_general(
+            unit_t[cols, :], w_all[...], NT, preferred_element_type=jnp.float32
+        )
+        ga = (ga * multiplier).T.astype(jnp.bfloat16)
+        for owner in range(n_blk):
+            ga_stage[owner % 2, owner // 2, :, cols] = ga[owner * own_att:(owner + 1) * own_att, :]
+        return carry
+
+    lax.fori_loop(0, PARTS, att_third, 0)
     ga_copy = send(ga_stage.at[1 - core], ga_core, {"blk": sibling})
     add_sibling(PARTS - 1)
     advance(PARTS - 1)

time: 50.1 us -> 48.5 us (0.968)
  Pallas kernels: 49.3 us -> 47.7 us
    pallas_call x1, Pallas kernels: 47.8 us -> 46.2 us  [on_device(): pl.pallas_call(functools.partial(kernel, n_grp, n_blk, plan, chunk), out_...]
where the time goes in v5:
time: 48.5 us; the launch traced here: 48.4 us
  Pallas kernels  47.7 us (98%)
  between operations  0.64 us (1%)
    pallas_call x1, Pallas kernels, on_device(): pl.pallas_call(functools.partial(kernel, n_grp, n_blk, plan, chunk), out_...  46.2 us
    pallas_call x1, Pallas kernels, on_device(): pl.pallas_call(write_out, out_shape=(jax.ShapeDtypeStruct((1, queries), f...  1.51 us

profile of v5, /device:TPU:1, one launch (start us, length us, event | category | flops | bytes accessed | tf_op | source)
XLA Modules:
  0.0 48.4 jit_solution(17632602669889648994)
XLA Ops:
  0.6 46.2 %shard_map.76 = (f32[1,2048]{1,0:T(1,128)S(1)}, f32[64,768]{1,0:T(8,128)S(1)}, bf16[2,3,768,128]{3,2,1,0:T(8,128)(2,1)S(1)}) custom-call(bf16[2048,768]{1,0:T(8,128)(2,1)} %states_hbm.1, bf16[768,768]{1,0:T(8,128)(2,1)} %weight_hbm.1, bf16[64,768]{1,0:T(8,128)(2,1)} %attempts_hbm.1, s32[1,256]{1,0:T(1,128)} %bitcast.4, s32[1,2048]{1,0:T(1,128)} %bitcast.3), custom_call_target="tpu_custom_call" | custom-call | tf_op jit(solution)/shard_map/pallas_call | solution.py:395
  46.9 1.5 %shard_map.77 = (f32[1,2048]{1,0:T(1,128)}, f32[64,768]{1,0:T(8,128)}, f32[768,768]{1,0:T(8,128)}) custom-call(f32[1,2048]{1,0:T(1,128)S(1)} %get-tuple-element.9.loss, f32[64,768]{1,0:T(8,128)S(1)} %get-tuple-element.10.grad_att, bf16[2,3,768,128]{3,2,1,0:T(8,128)(2,1)S(1)} %get-tuple-element.11.res), custom_call_target="tpu_custom_call" | custom-call | tf_op jit(solution)/shard_map/pallas_call | solution.py:433

commit v6 on v3

--- a/solution.py
+++ b/solution.py
@@ -20,9 +20,9 @@
     along_x = ("blk", 2, n_blk // 2)
     along_y = ("grp", 1, 2)
     along_z = ("grp", 2, n_grp // 2)
-    xyz, yxz, zxy = (along_x, along_y, along_z), (along_y, along_x, along_z), (along_z, along_x, along_y)
+    xyz, yxz = (along_x, along_y, along_z), (along_y, along_x, along_z)
     pieces = []
-    split = (((zxy, 1), (xyz, 1), (yxz, 1)), ((xyz, 2), (yxz, 1)), ((xyz, 1), (yxz, 2)))
+    split = (((xyz, 3),), ((yxz, 3),), ((xyz, 2), (yxz, 1)))
     for block, row in enumerate(split):
         first = 0
         for order, count in row:
@@ -59,7 +59,6 @@
     core = lax.rem(blk, 2)
     sibling = blk + 1 - 2 * core
     used = [0]
-    started = []
 
     def member(axis, stride, size):
         index = grp if axis == "grp" else blk
@@ -79,7 +78,6 @@
             device_id=device, device_id_type=MESH,
         )
         copy.start()
-        started.append(copy)
         return copy
 
     def load(src, dst, n):
@@ -142,14 +140,14 @@
     steps = queries // chunk
     lax.fori_loop(0, steps // 2, project, 0)
     for k, copy in enumerate(across):
-        copy.wait_recv()
+        copy.wait()
         source = lax.rem(blk // 2 + n_blk // 2 - (k + 1), n_blk // 2) * 2 + core
         rows = pl.ds(pl.multiple_of(source * own_att, own_att), own_att)
         to_sibling.append(send(panel.at[rows], panel.at[rows], {"blk": sibling}))
     lax.fori_loop(steps // 2, steps, project, 0)
 
     for copy in to_sibling:
-        copy.wait_recv()
+        copy.wait()
     loads[2].wait()
     loads[3].wait()
     panel_t[...] = panel[...].T
@@ -203,7 +201,7 @@
         stage, recv = bufs[piece][j]
         here = member(axis, stride, size)
         for copy in pending[piece]:
-            copy.wait_recv()
+            copy.wait()
         if scatter:
             part = length // size
             begin[piece] = begin[piece] + here * part
@@ -247,11 +245,11 @@
                 start_back(piece, j)
                 yield
                 for copy in pending[piece]:
-                    copy.wait_recv()
+                    copy.wait()
         spot = res.at[core, block, pl.ds(first, rows)]
         pending[piece] = [send(spot, spot, {"blk": sibling})]
         yield
-        pending[piece][0].wait_recv()
+        pending[piece][0].wait()
 
     runs = [steps_of(piece) for piece in range(len(plan))]
 
@@ -292,7 +290,7 @@
                 core_copies.append(send(core_send.at[block], core_recv.at[block], {"blk": sibling}))
 
     def add_sibling(block):
-        core_copies[block].wait_recv()
+        core_copies[block].wait()
         acc[block] += core_recv[block].astype(jnp.float32)
 
     for block in range(PARTS):
@@ -316,7 +314,7 @@
     advance(1)
     advance(0)
 
-    ga_copy.wait_recv()
+    ga_copy.wait()
     ga_sum[...] = (
         ga_stage[core].astype(jnp.float32) + ga_core[...].astype(jnp.float32)
     ).astype(jnp.bfloat16)
@@ -332,7 +330,7 @@
     advance(1)
     advance(0)
     for copy in ga_copies:
-        copy.wait_recv()
+        copy.wait()
     ga = ga_stage[core, blk // 2].astype(jnp.float32) + ga_core[blk // 2].astype(jnp.float32)
     for k in range(n_blk // 2 - 1):
         ga = ga + ga_recv[k].astype(jnp.float32)
@@ -344,8 +342,6 @@
     more = True
     while more:
         more = any([advance(block) for block in (2, 1, 0)])
-    for copy in started:
-        copy.wait_send()
 
 
 def write_out(loss, grad_att, res, loss_hbm, grad_att_hbm, grad_w_hbm, wide, sems):

time: 47.3 us -> 47 us (level)
  no operation moved by 1% of the time
where the time goes in v6:
time: 47 us; the launch traced here: 46.7 us
  Pallas kernels  46.1 us (98%)
  between operations  0.64 us (1%)
    pallas_call x1, Pallas kernels, on_device(): pl.pallas_call(functools.partial(kernel, n_grp, n_blk, plan, chunk), out_...  44.6 us
    pallas_call x1, Pallas kernels, on_device(): pl.pallas_call(write_out, out_shape=(jax.ShapeDtypeStruct((1, queries), f...  1.53 us

profile of v6, /device:TPU:1, one launch (start us, length us, event | category | flops | bytes accessed | tf_op | source)
XLA Modules:
  0.0 46.7 jit_solution(6601722861832630731)
XLA Ops:
  0.6 44.6 %shard_map.76 = (f32[1,2048]{1,0:T(1,128)S(1)}, f32[64,768]{1,0:T(8,128)S(1)}, bf16[2,3,768,128]{3,2,1,0:T(8,128)(2,1)S(1)}) custom-call(bf16[2048,768]{1,0:T(8,128)(2,1)} %states_hbm.1, bf16[768,768]{1,0:T(8,128)(2,1)} %weight_hbm.1, bf16[64,768]{1,0:T(8,128)(2,1)} %attempts_hbm.1, s32[1,256]{1,0:T(1,128)} %bitcast.4, s32[1,2048]{1,0:T(1,128)} %bitcast.3), custom_call_target="tpu_custom_call" | custom-call | tf_op jit(solution)/shard_map/pallas_call | solution.py:397
  45.2 1.5 %shard_map.77 = (f32[1,2048]{1,0:T(1,128)}, f32[64,768]{1,0:T(8,128)}, f32[768,768]{1,0:T(8,128)}) custom-call(f32[1,2048]{1,0:T(1,128)S(1)} %get-tuple-element.9.loss, f32[64,768]{1,0:T(8,128)S(1)} %get-tuple-element.10.grad_att, bf16[2,3,768,128]{3,2,1,0:T(8,128)(2,1)S(1)} %get-tuple-element.11.res), custom_call_target="tpu_custom_call" | custom-call | tf_op jit(solution)/shard_map/pallas_call | solution.py:436

commit v7 on v6

--- a/solution.py
+++ b/solution.py
@@ -45,7 +45,7 @@
     states_hbm, weight_hbm, attempts_hbm, theorem_hbm, positive_hbm,
     loss, grad_att, res,
     states, weight, attempts, theorem, positive, load_sems,
-    weight_t, unit_t, gproj_t, w_all, inv_rms, along_all, panel, panel_t,
+    weight_t, proj_t, gproj_t, w_all, w_scaled, inv_rms, along_all, panel, panel_t,
     ga_stage, ga_core, ga_sum, ga_recv, acc, core_send, core_recv, send_sems, recv_sems, *stage_bufs,
 ):
     queries, dim = states.shape
@@ -134,7 +134,7 @@
         )
         r = lax.rsqrt(jnp.sum(proj * proj, axis=0, keepdims=True) * (1.0 / dim) + epsilon)
         inv_rms[:, cols] = r
-        unit_t[:, cols] = (proj * r).astype(jnp.bfloat16)
+        proj_t[:, cols] = proj.astype(jnp.bfloat16)
         return carry
 
     steps = queries // chunk
@@ -155,8 +155,9 @@
 
     def contrast(step, carry):
         cols = pl.ds(pl.multiple_of(step * chunk, chunk), chunk)
-        unit = unit_t[:, cols]
-        scores = jnp.dot(panel[...], unit, preferred_element_type=jnp.float32) * multiplier
+        r = inv_rms[:, cols]
+        scores = jnp.dot(panel[...], proj_t[:, cols], preferred_element_type=jnp.float32)
+        scores = scores * (r * multiplier)
         chosen = lax.broadcasted_iota(jnp.int32, scores.shape, 0) == positive[:, cols]
         label = jnp.sum(jnp.where(chosen, theorem_col, 0.0), axis=0, keepdims=True)
         expo = jnp.where(theorem_col == label, jnp.exp(scores), 0.0)
@@ -165,8 +166,9 @@
         loss[:, cols] = jnp.log(total) - pos_score
         w = (expo * (1.0 / total) - jnp.where(chosen, 1.0, 0.0)).astype(jnp.bfloat16)
         w_all[:, cols] = w
+        w_scaled[:, cols] = (w.astype(jnp.float32) * r).astype(jnp.bfloat16)
         along = jnp.sum(w.astype(jnp.float32) * scores, axis=0, keepdims=True) * (1.0 / dim)
-        along_all[:, cols] = along * inv_rms[:, cols]
+        along_all[:, cols] = along * r * r
         return carry
 
     lax.fori_loop(0, steps, contrast, 0)
@@ -268,7 +270,7 @@
         rows = slice(block * width, (block + 1) * width)
         g = jnp.dot(panel_t[rows, :], w_all[...], preferred_element_type=jnp.float32)
         gproj_t[rows, :] = (
-            g * (inv_rms[...] * multiplier) - unit_t[rows, :].astype(jnp.float32) * along_all[...]
+            g * (inv_rms[...] * multiplier) - proj_t[rows, :].astype(jnp.float32) * along_all[...]
         ).astype(jnp.bfloat16)
 
     def weight_third(block):
@@ -301,7 +303,7 @@
         weight_third(block)
 
     advance(0)
-    ga = lax.dot_general(unit_t[...], w_all[...], NT, preferred_element_type=jnp.float32)
+    ga = lax.dot_general(proj_t[...], w_scaled[...], NT, preferred_element_type=jnp.float32)
     ga = (ga * multiplier).T.astype(jnp.bfloat16)
     for owner in range(n_blk):
         ga_stage[owner % 2, owner // 2] = ga[owner * own_att:(owner + 1) * own_att, :]
@@ -414,6 +416,7 @@
             pltpu.VMEM((dim, queries), bf16),
             pltpu.VMEM((dim, queries), bf16),
             pltpu.VMEM((n_att, queries), bf16),
+            pltpu.VMEM((n_att, queries), bf16),
             pltpu.VMEM((1, queries), f32),
             pltpu.VMEM((1, queries), f32),
             pltpu.VMEM((n_att, dim), bf16),

time: 47 us -> 46.6 us (level)
  no operation moved by 1% of the time
where the time goes in v7:
time: 46.6 us; the launch traced here: 46.4 us
  Pallas kernels  45.7 us (98%)
  between operations  0.64 us (1%)
    pallas_call x1, Pallas kernels, on_device(): pl.pallas_call(functools.partial(kernel, n_grp, n_blk, plan, chunk), out_...  44.2 us
    pallas_call x1, Pallas kernels, on_device(): pl.pallas_call(write_out, out_shape=(jax.ShapeDtypeStruct((1, queries), f...  1.53 us

profile of v7, /device:TPU:1, one launch (start us, length us, event | category | flops | bytes accessed | tf_op | source)
XLA Modules:
  0.0 46.4 jit_solution(12983119783473965132)
XLA Ops:
  0.6 44.2 %shard_map.76 = (f32[1,2048]{1,0:T(1,128)S(1)}, f32[64,768]{1,0:T(8,128)S(1)}, bf16[2,3,768,128]{3,2,1,0:T(8,128)(2,1)S(1)}) custom-call(bf16[2048,768]{1,0:T(8,128)(2,1)} %states_hbm.1, bf16[768,768]{1,0:T(8,128)(2,1)} %weight_hbm.1, bf16[64,768]{1,0:T(8,128)(2,1)} %attempts_hbm.1, s32[1,256]{1,0:T(1,128)} %bitcast.4, s32[1,2048]{1,0:T(1,128)} %bitcast.3), custom_call_target="tpu_custom_call" | custom-call | tf_op jit(solution)/shard_map/pallas_call | solution.py:399
  44.8 1.5 %shard_map.77 = (f32[1,2048]{1,0:T(1,128)}, f32[64,768]{1,0:T(8,128)}, f32[768,768]{1,0:T(8,128)}) custom-call(f32[1,2048]{1,0:T(1,128)S(1)} %get-tuple-element.9.loss, f32[64,768]{1,0:T(8,128)S(1)} %get-tuple-element.10.grad_att, bf16[2,3,768,128]{3,2,1,0:T(8,128)(2,1)S(1)} %get-tuple-element.11.res), custom_call_target="tpu_custom_call" | custom-call | tf_op jit(solution)/shard_map/pallas_call | solution.py:439
